TPU v7x, 32 devices: a whole 2x2x4 slice. The times are simulated.
32 devices in a mesh: blk: 8 (over z, x), rep: 4 (over y, core).
Axes of the slice: x: 2, y: 2, z: 4, core: 2. Of those that a mesh axis runs over, the one named last changes fastest.
Arguments:
- pixel_factors: float32 [24576, 256], P(('blk', 'rep')), may hold values from -1.5 to 1.5
- scene_factors: float32 [8192, 256], P('blk'), may hold values from -1.5 to 1.5
- elevations: bfloat16 [3, 24576, 1024], P(None, ('blk', 'rep')), may hold values from -6 to 6
- quality: bfloat16 [3, 24576, 1024], P(None, ('blk', 'rep')), may hold values from 0 to 1, as said below
- occupancy: int32 [3, 32], P(None, ('blk', 'rep')), may hold values from 0 to 1, as said below
Outputs:
- pixel_out: float32 [24576, 256], P(('blk', 'rep'))
- scene_out: float32 [8192, 256], P('blk')
Inputs may be any that keep to these rules, and one draw needn't show every extreme that they name: quality is zero on every entry of an owner's tile whose occupancy is 0; otherwise about half of the entries are nonzero. occupancy is 0 or 1 and about three quarters of the tiles are occupied.
All inputs are finite; a program needn't handle non-finite values.
Results may differ from a plain program's by a relative error of at most 0.0003.
Values sent between devices are 32-bit elements; how exact they have to be, the bound alone decides.
A program may use at most 64 MiB of HBM per device.

v0:
```python
import jax
import jax.numpy as jnp
from jax import lax
from jax.sharding import PartitionSpec as P

ACQ_BLK = 1024
STEPS = 3


def shifted(value, axis, steps):
    count = lax.axis_size(axis)
    pairs = [(source, (source + steps) % count) for source in range(count)]
    return lax.ppermute(value, axis, pairs)


def tile_gradients(pixel_rows, scene_block, tile_values, weight):
    predicted = lax.dot_general(
        pixel_rows,
        scene_block,
        (((1,), (1,)), ((), ())),
        precision=lax.Precision.HIGHEST,
        preferred_element_type=jnp.float32,
    )
    misfit = weight * (tile_values.astype(jnp.float32) - predicted)
    pixel_grad = jnp.dot(
        misfit, scene_block, precision=lax.Precision.HIGHEST, preferred_element_type=jnp.float32
    )
    scene_grad = lax.dot_general(
        misfit,
        pixel_rows,
        (((0,), (0,)), ((), ())),
        precision=lax.Precision.HIGHEST,
        preferred_element_type=jnp.float32,
    )
    return (pixel_grad, scene_grad)


def per_device(pixel_factors, scene_factors, elevations, quality, occupancy):
    pixel_rows = pixel_factors
    scene_block = scene_factors
    rep_count = lax.axis_size("rep")
    group_rows = pixel_rows.shape[0] * rep_count
    share_rows = scene_block.shape[0] // rep_count
    share_start = lax.axis_index("rep") * share_rows
    for step_index in range(STEPS):
        flag = occupancy[step_index, 0]
        weight = quality[step_index].astype(jnp.float32) * flag.astype(jnp.float32)
        pixel_grad, scene_grad = tile_gradients(
            pixel_rows, scene_block, elevations[step_index], weight
        )
        pixel_rows = pixel_rows + 8.0 / ACQ_BLK * pixel_grad
        grad_share = lax.psum_scatter(scene_grad, "rep", scatter_dimension=0, tiled=True)
        own_rows = lax.dynamic_slice_in_dim(scene_block, share_start, share_rows, 0)
        own_rows = own_rows + 8.0 / group_rows * grad_share
        if step_index + 1 < STEPS:
            own_rows = shifted(own_rows, "blk", -1)
        else:
            own_rows = shifted(own_rows, "blk", STEPS - 1)
        scene_block = lax.all_gather(own_rows, "rep", axis=0, tiled=True)
    return (pixel_rows, scene_block)


def solution(mesh):
    in_specs = (
        P(("blk", "rep"), None),
        P("blk", None),
        P(None, ("blk", "rep"), None),
        P(None, ("blk", "rep"), None),
        P(None, ("blk", "rep")),
    )
    out_specs = (P(("blk", "rep"), None), P("blk", None))
    return jax.shard_map(
        per_device, mesh=mesh, in_specs=in_specs, out_specs=out_specs, check_vma=False
    )
```

profile of v0, /device:TPU:1, one launch (start us, length us, event | category | flops | bytes accessed | tf_op | source)
XLA Modules:
  0.0 216.9 jit_solution(5446831069889582421)
XLA Ops:
  7.2 0.0 reduce-scatter.4.cloned.1.call-start
  7.2 1.4 fusion.6
  9.3 0.0 copy-start.2
  9.3 5.5 %fusion.2 = f32[768,1024]{1,0:T(8,128)S(1)} fusion(f32[768,256]{1,0:T(8,128)} %param.5, f32[1024,256]{1,0:T(8,128)} %param.6, bf16[3,768,1024]{2,1,0:T(8,128)(2,1)} %param.7, f32[]{:T(128)} %bitcast, bf16[3,768,1024]{2,1,0:T(8,128)(2,1)} %param.8), kind=kOutput, calls=%fused_computation.5 | convolution fusion | flops 2419851264 | bytes 8126468 | tf_op jit(solution)/shard_map/dot_general | solution.py:17
  14.8 0.0 copy-done.2
  14.8 6.1 %fusion.7 = f32[1024,256]{1,0:T(8,128)} fusion(f32[768,1024]{1,0:T(8,128)S(1)} %fusion.2, f32[768,256]{1,0:T(8,128)S(1)} %copy-done.2), kind=kOutput, calls=%fused_computation.16 | convolution fusion | flops 2415919104 | bytes 4980736 | tf_op jit(solution)/shard_map/dot_general | solution.py:28
  20.9 0.0 reduce-scatter.4.cloned.1.call-update
  20.9 0.0 all-gather.4.cloned.1.call-start
  21.0 27.1 %reduce-scatter.4.cloned.1.call-done = f32[256,256]{1,0:T(8,128)} async-done(((f32[1024,256]{1,0:T(8,128)}), f32[256,256]{1,0:T(8,128)}) %reduce-scatter.4.cloned.1.call-update) | async-done | bytes 262160 | tf_op jit(solution)/shard_map/reduce_scatter | solution.py:52
  48.0 1.1 multiply_add_fusion.2
  49.1 4.0 %collective-permute-start = (f32[256,256]{1,0:T(8,128)S(1)}, f32[256,256]{1,0:T(8,128)S(1)}, u32[]{:S(2)}, u32[]{:S(2)}) collective-permute-start(f32[256,256]{1,0:T(8,128)S(1)} %multiply_add_fusion.2), channel_id=1, source_target_pairs={{0,28},{4,0},{8,4},{12,8},{16,12},{20,16},{24,20},{28,24},{1,29},{... | collective-permute-start | bytes 786440 | tf_op jit(solution)/shard_map/ppermute | solution.py:13
  53.1 5.0 %collective-permute-done = f32[256,256]{1,0:T(8,128)S(1)} collective-permute-done((f32[256,256]{1,0:T(8,128)S(1)}, f32[256,256]{1,0:T(8,128)S(1)}, u32[]{:S(2)}, u32[]{:S(2)}) %collective-permute-start) | collective-permute-done | bytes 262176 | tf_op jit(solution)/shard_map/ppermute | solution.py:13
  58.1 0.0 copy-start.4
  58.1 0.7 copy-done.4
  58.8 0.0 all-gather.4.cloned.1.call-update
  58.8 0.2 reduce-scatter.6.cloned.1.call-start
  59.7 4.9 %fusion.5 = f32[768,256]{1,0:T(8,128)} fusion(f32[768,256]{1,0:T(8,128)} %param.5, f32[768,1024]{1,0:T(8,128)S(1)} %fusion.2, f32[1024,256]{1,0:T(8,128)} %param.6), kind=kOutput, calls=%fused_computation.11 | convolution fusion | flops 2416312320 | bytes 5767168 | tf_op jit(solution)/shard_map/dot_general | solution.py:25
  64.6 13.3 %all-gather.4.cloned.1.call-done = f32[1024,256]{1,0:T(8,128)} async-done(((f32[256,256]{1,0:T(8,128)}), f32[1024,256]{1,0:T(8,128)}) %all-gather.4.cloned.1.call-update) | async-done | bytes 1048592 | tf_op jit(solution)/shard_map/all_gather | solution.py:59
  77.9 0.0 copy-start
  77.9 5.5 %fusion.1 = f32[768,1024]{1,0:T(8,128)S(1)} fusion(f32[768,256]{1,0:T(8,128)} %fusion.5, f32[1024,256]{1,0:T(8,128)} %all-gather.4.cloned.1.call-done, bf16[3,768,1024]{2,1,0:T(8,128)(2,1)} %param.7, f32[]{:T(128)} %bitcast.3, bf16[3,768,1024]{2,1,0:T(8,128)(2,1)} %param.8), kind=kOutput, calls=%fused_computation.3 | convolution fusion | flops 2419851264 | bytes 8126468 | tf_op jit(solution)/shard_map/dot_general | solution.py:17
  83.5 0.0 copy-done
  83.5 6.1 %fusion.8 = f32[1024,256]{1,0:T(8,128)} fusion(f32[768,1024]{1,0:T(8,128)S(1)} %fusion.1, f32[768,256]{1,0:T(8,128)S(1)} %copy-done), kind=kOutput, calls=%fused_computation.17 | convolution fusion | flops 2415919104 | bytes 4980736 | tf_op jit(solution)/shard_map/dot_general | solution.py:28
  89.5 0.0 reduce-scatter.6.cloned.1.call-update
  89.5 0.0 all-gather.6.cloned.1.call-start
  89.6 24.6 %reduce-scatter.6.cloned.1.call-done = f32[256,256]{1,0:T(8,128)} async-done(((f32[1024,256]{1,0:T(8,128)}), f32[256,256]{1,0:T(8,128)}) %reduce-scatter.6.cloned.1.call-update) | async-done | bytes 262160 | tf_op jit(solution)/shard_map/reduce_scatter | solution.py:52
  114.2 1.1 multiply_add_fusion.1
  115.3 4.0 %collective-permute-start.1 = (f32[256,256]{1,0:T(8,128)S(1)}, f32[256,256]{1,0:T(8,128)S(1)}, u32[]{:S(2)}, u32[]{:S(2)}) collective-permute-start(f32[256,256]{1,0:T(8,128)S(1)} %multiply_add_fusion.1), channel_id=1, source_target_pairs={{0,28},{4,0},{8,4},{12,8},{16,12},{20,16},{24,20},{28,24},{1,29},{... | collective-permute-start | bytes 786440 | tf_op jit(solution)/shard_map/ppermute | solution.py:13
  119.3 5.0 %collective-permute-done.1 = f32[256,256]{1,0:T(8,128)S(1)} collective-permute-done((f32[256,256]{1,0:T(8,128)S(1)}, f32[256,256]{1,0:T(8,128)S(1)}, u32[]{:S(2)}, u32[]{:S(2)}) %collective-permute-start.1) | collective-permute-done | bytes 262176 | tf_op jit(solution)/shard_map/ppermute | solution.py:13
  124.3 0.0 copy-start.3
  124.3 0.7 copy-done.3
  125.0 0.0 all-gather.6.cloned.1.call-update
  125.0 0.3 reduce-scatter.8.cloned.1.call-start
  125.9 4.9 %fusion.4 = f32[768,256]{1,0:T(8,128)} fusion(f32[768,256]{1,0:T(8,128)} %fusion.5, f32[768,1024]{1,0:T(8,128)S(1)} %fusion.1, f32[1024,256]{1,0:T(8,128)} %all-gather.4.cloned.1.call-done), kind=kOutput, calls=%fused_computation.9 | convolution fusion | flops 2416312320 | bytes 5767168 | tf_op jit(solution)/shard_map/dot_general | solution.py:25
  130.9 13.2 %all-gather.6.cloned.1.call-done = f32[1024,256]{1,0:T(8,128)} async-done(((f32[256,256]{1,0:T(8,128)}), f32[1024,256]{1,0:T(8,128)}) %all-gather.6.cloned.1.call-update) | async-done | bytes 1048592 | tf_op jit(solution)/shard_map/all_gather | solution.py:59
  144.1 0.0 copy-start.1
  144.1 5.5 %fusion = f32[768,1024]{1,0:T(8,128)S(1)} fusion(f32[768,256]{1,0:T(8,128)} %fusion.4, f32[1024,256]{1,0:T(8,128)} %all-gather.6.cloned.1.call-done, bf16[3,768,1024]{2,1,0:T(8,128)(2,1)} %param.7, f32[]{:T(128)} %bitcast.6, bf16[3,768,1024]{2,1,0:T(8,128)(2,1)} %param.8), kind=kOutput, calls=%fused_computation.1 | convolution fusion | flops 2419851264 | bytes 8126468 | tf_op jit(solution)/shard_map/dot_general | solution.py:17
  149.6 0.0 copy-done.1
  149.6 6.1 %fusion.9 = f32[1024,256]{1,0:T(8,128)} fusion(f32[768,1024]{1,0:T(8,128)S(1)} %fusion, f32[768,256]{1,0:T(8,128)S(1)} %copy-done.1), kind=kOutput, calls=%fused_computation.18 | convolution fusion | flops 2415919104 | bytes 4980736 | tf_op jit(solution)/shard_map/dot_general | solution.py:28
  155.7 0.0 reduce-scatter.8.cloned.1.call-update
  155.7 0.0 all-gather.8.cloned.1.call-start
  155.7 24.6 %reduce-scatter.8.cloned.1.call-done = f32[256,256]{1,0:T(8,128)} async-done(((f32[1024,256]{1,0:T(8,128)}), f32[256,256]{1,0:T(8,128)}) %reduce-scatter.8.cloned.1.call-update) | async-done | bytes 262160 | tf_op jit(solution)/shard_map/reduce_scatter | solution.py:52
  180.4 1.1 multiply_add_fusion
  181.4 1.5 collective-permute-start.2
  182.9 7.8 %collective-permute-done.2 = f32[256,256]{1,0:T(8,128)S(1)} collective-permute-done((f32[256,256]{1,0:T(8,128)S(1)}, f32[256,256]{1,0:T(8,128)S(1)}, u32[]{:S(2)}, u32[]{:S(2)}) %collective-permute-start.2) | collective-permute-done | bytes 262176 | tf_op jit(solution)/shard_map/ppermute | solution.py:13
  190.7 0.0 copy-start.5
  190.7 0.7 copy-done.5
  191.4 0.0 all-gather.8.cloned.1.call-update
  191.4 4.9 %fusion.3 = f32[768,256]{1,0:T(8,128)} fusion(f32[768,256]{1,0:T(8,128)} %fusion.4, f32[768,1024]{1,0:T(8,128)S(1)} %fusion, f32[1024,256]{1,0:T(8,128)} %all-gather.6.cloned.1.call-done), kind=kOutput, calls=%fused_computation.7 | convolution fusion | flops 2416312320 | bytes 5767168 | tf_op jit(solution)/shard_map/dot_general | solution.py:25
  196.4 11.4 %all-gather.8.cloned.1.call-done = f32[1024,256]{1,0:T(8,128)} async-done(((f32[256,256]{1,0:T(8,128)}), f32[1024,256]{1,0:T(8,128)}) %all-gather.8.cloned.1.call-update) | async-done | bytes 1048592 | tf_op jit(solution)/shard_map/all_gather | solution.py:59
  207.8 2.3 %copy.8 = f32[1024,256]{1,0:T(8,128)} copy(f32[1024,256]{1,0:T(8,128)} %all-gather.8.cloned.1.call-done) | data formatting | bytes 2097152
Async XLA Ops:
  7.2 40.9 %reduce-scatter.4.cloned.1.call-start = ((), (), s32[]{:S(2)}) async-start(), calls=%async_computation.3 | async-start | bytes 1310720 | tf_op jit(solution)/shard_map/reduce_scatter | solution.py:52
  9.3 5.5 %copy-start.2 = (f32[768,256]{1,0:T(8,128)S(1)}, f32[768,256]{1,0:T(8,128)}, u32[]{:S(2)}) copy-start(f32[768,256]{1,0:T(8,128)} %param.5) | copy-start | bytes 2359300
  20.9 57.0 %all-gather.4.cloned.1.call-start = ((), (), s32[]{:S(2)}) async-start(), calls=%async_computation.4 | async-start | bytes 1310720 | tf_op jit(solution)/shard_map/all_gather | solution.py:59
  49.1 9.0 %collective-permute-start = (f32[256,256]{1,0:T(8,128)S(1)}, f32[256,256]{1,0:T(8,128)S(1)}, u32[]{:S(2)}, u32[]{:S(2)}) collective-permute-start(f32[256,256]{1,0:T(8,128)S(1)} %multiply_add_fusion.2), channel_id=1, source_target_pairs={{0,28},{4,0},{8,4},{12,8},{16,12},{20,16},{24,20},{28,24},{1,29},{... | collective-permute-start | bytes 786440 | tf_op jit(solution)/shard_map/ppermute | solution.py:13
  58.1 0.7 copy-start.4
  58.8 55.4 %reduce-scatter.6.cloned.1.call-start = ((), (), s32[]{:S(2)}) async-start(), calls=%async_computation.5 | async-start | bytes 1310720 | tf_op jit(solution)/shard_map/reduce_scatter | solution.py:52
  77.9 5.5 %copy-start = (f32[768,256]{1,0:T(8,128)S(1)}, f32[768,256]{1,0:T(8,128)}, u32[]{:S(2)}) copy-start(f32[768,256]{1,0:T(8,128)} %fusion.5) | copy-start | bytes 2359300
  89.5 54.5 %all-gather.6.cloned.1.call-start = ((), (), s32[]{:S(2)}) async-start(), calls=%async_computation.6 | async-start | bytes 1310720 | tf_op jit(solution)/shard_map/all_gather | solution.py:59
  115.3 9.0 %collective-permute-start.1 = (f32[256,256]{1,0:T(8,128)S(1)}, f32[256,256]{1,0:T(8,128)S(1)}, u32[]{:S(2)}, u32[]{:S(2)}) collective-permute-start(f32[256,256]{1,0:T(8,128)S(1)} %multiply_add_fusion.1), channel_id=1, source_target_pairs={{0,28},{4,0},{8,4},{12,8},{16,12},{20,16},{24,20},{28,24},{1,29},{... | collective-permute-start | bytes 786440 | tf_op jit(solution)/shard_map/ppermute | solution.py:13
  124.3 0.7 copy-start.3
  125.0 55.4 %reduce-scatter.8.cloned.1.call-start = ((), (), s32[]{:S(2)}) async-start(), calls=%async_computation.7 | async-start | bytes 1310720 | tf_op jit(solution)/shard_map/reduce_scatter | solution.py:52
  144.1 5.5 %copy-start.1 = (f32[768,256]{1,0:T(8,128)S(1)}, f32[768,256]{1,0:T(8,128)}, u32[]{:S(2)}) copy-start(f32[768,256]{1,0:T(8,128)} %fusion.4) | copy-start | bytes 2359300
  155.7 52.1 %all-gather.8.cloned.1.call-start = ((), (), s32[]{:S(2)}) async-start(), calls=%async_computation.8 | async-start | bytes 1310720 | tf_op jit(solution)/shard_map/all_gather | solution.py:59
  181.4 9.3 %collective-permute-start.2 = (f32[256,256]{1,0:T(8,128)S(1)}, f32[256,256]{1,0:T(8,128)S(1)}, u32[]{:S(2)}, u32[]{:S(2)}) collective-permute-start(f32[256,256]{1,0:T(8,128)S(1)} %multiply_add_fusion), channel_id=1, source_target_pairs={{0,8},{4,12},{8,16},{12,20},{16,24},{20,28},{24,0},{28,4},{1,9},{5... | collective-permute-start | bytes 786440 | tf_op jit(solution)/shard_map/ppermute | solution.py:13
  190.7 0.7 copy-start.5
Sparse Core Ops, SparseCore 0:
  21.0 26.9 reduce-scatter.3
  58.9 18.9 all-gather.3
  89.7 24.4 reduce-scatter.5
  125.1 18.9 all-gather.5
  155.8 24.4 reduce-scatter.7
  191.6 16.1 all-gather.7
where the time goes:
time: 217 us
  waiting for transfers between devices  132 us (61%)
  matrix products  49.6 us (23%)
  between operations  16.1 us (7%)
  starting transfers between devices  10.2 us (5%)
  local copies, waits for them, and re-layouts  5.8 us (3%)
  other arithmetic  3.19 us (1%)
    reduce_scatter x3, waiting for transfers between devices, per_device(): lax.psum_scatter(scene_grad, 'rep', scatter_dimension=0, tiled=True)  76.3 us
    all_gather x3, waiting for transfers between devices, per_device(): scene_block = lax.all_gather(own_rows, 'rep', axis=0, tiled=True)  37.9 us
    dot_general x3, matrix products, tile_gradients(): lax.dot_general(misfit, pixel_rows, (((0,), (0,)), ((), ())), precision=l...  18.2 us
    ppermute x3, waiting for transfers between devices, shifted(): return lax.ppermute(value, axis, pairs)  17.7 us
    dot_general x3, matrix products, tile_gradients(): lax.dot_general(pixel_rows, scene_block, (((1,), (1,)), ((), ())), precis...  16.6 us
    dot_general x3, matrix products, tile_gradients(): jnp.dot(misfit, scene_block, precision=lax.Precision.HIGHEST, preferred_e...  14.8 us
    ppermute x3, starting transfers between devices, shifted(): return lax.ppermute(value, axis, pairs)  9.56 us
    unnamed x13, local copies, waits for them, and re-layouts  4.38 us
  transfers between devices with their start and end apart: 9, of which 9 were waited for; matrix products, arithmetic and copies ran while one was open for 7% of the time, Pallas kernels for 0%

commit v1 on v0

v1 whole, which is shorter than its diff:
```python
import functools

import jax
import jax.numpy as jnp
from jax import lax
from jax.experimental import pallas as pl
from jax.experimental.pallas import tpu as pltpu
from jax.sharding import PartitionSpec as P

MESH = pl.DeviceIdType.MESH
STEPS = 3
CHUNK = 128
PAIR = 256
ROWS = 256
LAG_SUM = 1
LAG_UPDATE = 3
LAG_FORWARD = 5


def split(value):
    high = value.astype(jnp.bfloat16)
    return high, (value - high.astype(jnp.float32)).astype(jnp.bfloat16)


def dot(left, right):
    return jnp.dot(left, right, preferred_element_type=jnp.float32)


def kernel(
    blk_count, rep_count,
    occ_ref, pix_ref, scene_ref, elev_ref, qual_ref, pix_out, scene_out,
    elev, qual, u_ref, p_ref, u_cat, ut_high, ut_low, v_all, v_high, v_low, m_high, m_low,
    grad, core_in, chip_sum, fresh,
    load_sem, tile_sem, core_send, core_recv, chip_send, chip_recv, move_send, move_recv, fwd_send, fwd_recv,
):
    pixels, rank = pix_ref.shape
    acq = scene_ref.shape[0]
    per_step = acq // CHUNK
    total = STEPS * per_step
    half = CHUNK // 2
    chips = rep_count // 2
    pixel_rate = 8.0 / acq
    scene_rate = 8.0 / (pixels * rep_count)

    group = lax.axis_index("blk")
    rep = lax.axis_index("rep")
    core = lax.rem(rep, 2)
    chip = lax.div(rep, 2)
    other_core = chip * 2 + 1 - core

    load_u = pltpu.make_async_copy(pix_ref, u_ref, load_sem.at[0])
    load_v = pltpu.make_async_copy(scene_ref, v_all.at[0], load_sem.at[1])
    load_u.start()
    load_v.start()

    def tile_loads(step):
        return (
            pltpu.make_async_copy(elev_ref.at[step], elev.at[step], tile_sem.at[0, step]),
            pltpu.make_async_copy(qual_ref.at[step], qual.at[step], tile_sem.at[1, step]),
        )

    for step in range(STEPS):
        for load in tile_loads(step):
            load.start()

    def at_blk(shift):
        return lax.rem(group + shift + blk_count, blk_count)

    barrier = pltpu.get_barrier_semaphore()
    partners = [(group, other_core)]
    for offset in range(1, chips):
        partners.append((group, lax.rem(chip + offset, chips) * 2 + core))
    for shift in (-1, 1, STEPS - 1, 1 - STEPS):
        partners.append((at_blk(shift), rep))
    for partner in partners:
        pl.semaphore_signal(barrier, inc=1, device_id=partner, device_id_type=MESH)

    p_ref[...] = jnp.zeros_like(p_ref)
    load_u.wait()
    load_v.wait()
    pl.semaphore_wait(barrier, len(partners))

    def core_copy(n):
        return pltpu.make_async_remote_copy(
            src_ref=grad.at[n, pl.ds(pl.multiple_of((1 - core) * half, half), half)],
            dst_ref=core_in.at[n],
            send_sem=core_send.at[n], recv_sem=core_recv.at[n],
            device_id=(group, other_core), device_id_type=MESH,
        )

    def chip_copy(n, offset):
        return pltpu.make_async_remote_copy(
            src_ref=chip_sum.at[n, chip], dst_ref=chip_sum.at[n, chip],
            send_sem=chip_send.at[n, offset - 1], recv_sem=chip_recv.at[n, chip],
            device_id=(group, lax.rem(chip + offset, chips) * 2 + core), device_id_type=MESH,
        )

    def chip_arrival(n, offset):
        sender = lax.rem(chip + offset, chips)
        return pltpu.make_async_remote_copy(
            src_ref=chip_sum.at[n, sender], dst_ref=chip_sum.at[n, sender],
            send_sem=chip_send.at[n, offset - 1], recv_sem=chip_recv.at[n, sender],
            device_id=(group, sender * 2 + core), device_id_type=MESH,
        )

    def place(n, side):
        step = lax.div(n, per_step)
        start = lax.rem(n, per_step) * CHUNK + side * half
        return v_all.at[step + 1, pl.ds(pl.multiple_of(start, half), half)]

    def move_copy(n):
        last = lax.div(lax.div(n, per_step), STEPS - 1)
        return pltpu.make_async_remote_copy(
            src_ref=fresh.at[n], dst_ref=place(n, core),
            send_sem=move_send.at[n], recv_sem=move_recv.at[n],
            device_id=(at_blk(last * STEPS - 1), rep), device_id_type=MESH,
        )

    def forward_copy(n):
        return pltpu.make_async_remote_copy(
            src_ref=place(n, core), dst_ref=place(n, core),
            send_sem=fwd_send.at[n], recv_sem=fwd_recv.at[n],
            device_id=(group, other_core), device_id_type=MESH,
        )

    def forward_arrival(n):
        return pltpu.make_async_remote_copy(
            src_ref=place(n, 1 - core), dst_ref=place(n, 1 - core),
            send_sem=fwd_send.at[n], recv_sem=fwd_recv.at[n],
            device_id=(group, other_core), device_id_type=MESH,
        )

    def begin_step(step):
        for load in tile_loads(step):
            load.wait()
        for start in range(0, pixels, ROWS):
            rows = pl.ds(start, ROWS)
            u = u_ref[rows, :] + pixel_rate * p_ref[rows, :]
            u_ref[rows, :] = u
            p_ref[rows, :] = jnp.zeros_like(u)
            high, low = split(u)
            u_cat[rows, :] = jnp.concatenate([high, high, low], axis=1)
            high, low = split(u.T)
            ut_high[:, rows] = high
            ut_low[:, rows] = low

    def work(n):
        step = lax.div(n, per_step)
        first = pl.multiple_of(lax.rem(n, per_step) * CHUNK, CHUNK)
        cols = pl.ds(first, CHUNK)
        flag = occ_ref[step, 0].astype(jnp.float32)
        v = v_all[step, cols, :]
        high, low = split(v)
        v_high[cols, :] = high
        v_low[cols, :] = low
        high, low = split(v.T)
        v_cat = jnp.concatenate([high, low, high], axis=0)
        for start in range(0, pixels, ROWS):
            rows = pl.ds(start, ROWS)
            predicted = dot(u_cat[rows, :], v_cat)
            weight = qual[step, rows, cols].astype(jnp.float32) * flag
            misfit = weight * (elev[step, rows, cols].astype(jnp.float32) - predicted)
            high, low = split(misfit)
            m_high[rows, cols] = high
            m_low[rows, cols] = low
        high = m_high[:, cols]
        turned = dot(ut_high[...], high) + dot(ut_high[...], m_low[:, cols]) + dot(ut_low[...], high)
        grad[n] = turned.T

    def add_pixel_grad(n):
        first = pl.multiple_of(lax.rem(n, per_step) * CHUNK + CHUNK - PAIR, PAIR)
        cols = pl.ds(first, PAIR)
        high, low = v_high[cols, :], v_low[cols, :]
        v_cat = jnp.concatenate([high, high, low], axis=0)
        for start in range(0, pixels, ROWS):
            rows = pl.ds(start, ROWS)
            high, low = m_high[rows, cols], m_low[rows, cols]
            p_ref[rows, :] += dot(jnp.concatenate([high, low, high], axis=1), v_cat)

    def tick(t, carry):
        @pl.when(t < total)
        def _():
            @pl.when(lax.rem(t, per_step) == 0)
            def _():
                begin_step(lax.div(t, per_step))

            @pl.when(t >= per_step)
            def _():
                forward_arrival(t - per_step).wait_recv()

            work(t)
            core_copy(t).start()

            @pl.when(lax.rem(lax.rem(t, per_step) * CHUNK + CHUNK, PAIR) == 0)
            def _():
                add_pixel_grad(t)

        n_sum = t - LAG_SUM

        @pl.when(jnp.logical_and(n_sum >= 0, n_sum < total))
        def _():
            core_copy(n_sum).wait_recv()
            own = grad[n_sum, pl.ds(pl.multiple_of(core * half, half), half), :]
            chip_sum[n_sum, chip] = own + core_in[n_sum]
            for offset in range(1, chips):
                chip_copy(n_sum, offset).start()

        n_new = t - LAG_UPDATE

        @pl.when(jnp.logical_and(n_new >= 0, n_new < total))
        def _():
            for offset in range(1, chips):
                chip_arrival(n_new, offset).wait_recv()
            summed = chip_sum[n_new, 0]
            for index in range(1, chips):
                summed = summed + chip_sum[n_new, index]
            start = lax.rem(n_new, per_step) * CHUNK + core * half
            old = v_all[lax.div(n_new, per_step), pl.ds(pl.multiple_of(start, half), half), :]
            fresh[n_new] = old + scene_rate * summed
            move_copy(n_new).start()

        n_fwd = t - LAG_FORWARD

        @pl.when(jnp.logical_and(n_fwd >= 0, n_fwd < total))
        def _():
            move_copy(n_fwd).wait_recv()
            forward_copy(n_fwd).start()

        return carry

    lax.fori_loop(0, total + LAG_FORWARD, tick, 0)

    for start in range(0, pixels, ROWS):
        rows = pl.ds(start, ROWS)
        pix_out[rows, :] = u_ref[rows, :] + pixel_rate * p_ref[rows, :]

    def finish(c, carry):
        forward_arrival((STEPS - 1) * per_step + c).wait_recv()
        cols = pl.ds(pl.multiple_of(c * CHUNK, CHUNK), CHUNK)
        scene_out[cols, :] = v_all[STEPS, cols, :]
        return carry

    lax.fori_loop(0, per_step, finish, 0)

    def drain(n, carry):
        core_copy(n).wait_send()
        for offset in range(1, chips):
            chip_copy(n, offset).wait_send()
        move_copy(n).wait_send()
        forward_copy(n).wait_send()
        return carry

    lax.fori_loop(0, total, drain, 0)


def per_device(blk_count, rep_count, pixel_factors, scene_factors, elevations, quality, occupancy):
    pixels, rank = pixel_factors.shape
    acq = scene_factors.shape[0]
    total = STEPS * (acq // CHUNK)
    half = CHUNK // 2
    chips = rep_count // 2
    f32, bf16 = jnp.float32, jnp.bfloat16
    anywhere = pl.BlockSpec(memory_space=pl.ANY)
    in_vmem = pl.BlockSpec(memory_space=pltpu.VMEM)
    dma = pltpu.SemaphoreType.DMA
    return pl.pallas_call(
        functools.partial(kernel, blk_count, rep_count),
        out_shape=(
            jax.ShapeDtypeStruct((pixels, rank), f32),
            jax.ShapeDtypeStruct((acq, rank), f32),
        ),
        in_specs=[pl.BlockSpec(memory_space=pltpu.SMEM)] + [anywhere] * 4,
        out_specs=(in_vmem, in_vmem),
        scratch_shapes=[
            pltpu.VMEM(elevations.shape, bf16),
            pltpu.VMEM(quality.shape, bf16),
            pltpu.VMEM((pixels, rank), f32),
            pltpu.VMEM((pixels, rank), f32),
            pltpu.VMEM((pixels, 3 * rank), bf16),
            pltpu.VMEM((rank, pixels), bf16),
            pltpu.VMEM((rank, pixels), bf16),
            pltpu.VMEM((STEPS + 1, acq, rank), f32),
            pltpu.VMEM((acq, rank), bf16),
            pltpu.VMEM((acq, rank), bf16),
            pltpu.VMEM((pixels, acq), bf16),
            pltpu.VMEM((pixels, acq), bf16),
            pltpu.VMEM((total, CHUNK, rank), f32),
            pltpu.VMEM((total, half, rank), f32),
            pltpu.VMEM((total, chips, half, rank), f32),
            pltpu.VMEM((total, half, rank), f32),
            dma((2,)),
            dma((2, STEPS)),
            dma((total,)),
            dma((total,)),
            dma((total, chips)),
            dma((total, chips)),
            dma((total,)),
            dma((total,)),
            dma((total,)),
            dma((total,)),
        ],
        compiler_params=pltpu.CompilerParams(
            collective_id=0, has_side_effects=True, vmem_limit_bytes=56 * 1024 * 1024
        ),
        cost_estimate=pl.CostEstimate(
            flops=18 * STEPS * pixels * acq * rank, bytes_accessed=12 * 1024 * 1024, transcendentals=0
        ),
    )(occupancy, pixel_factors, scene_factors, elevations, quality)


def solution(mesh):
    in_specs = (
        P(("blk", "rep"), None),
        P("blk", None),
        P(None, ("blk", "rep"), None),
        P(None, ("blk", "rep"), None),
        P(None, ("blk", "rep")),
    )
    out_specs = (P(("blk", "rep"), None), P("blk", None))
    return jax.shard_map(
        functools.partial(per_device, mesh.shape["blk"], mesh.shape["rep"]),
        mesh=mesh, in_specs=in_specs, out_specs=out_specs, check_vma=False,
    )
```

time: 217 us -> 70.4 us (0.32)
  waiting for transfers between devices: 132 us -> 0 us
  Pallas kernels: 0 us -> 63.9 us
  matrix products: 49.6 us -> 0 us
  between operations: 16.1 us -> 0.64 us
  starting transfers between devices: 10.2 us -> 0 us
  other arithmetic: 3.19 us -> 0 us
    reduce_scatter x3 -> x0, waiting for transfers between devices: 76.3 us -> none  [per_device(): lax.psum_scatter(scene_grad, 'rep', scatter_dimension=0, tiled=True)]
    pallas_call x0 -> x1, Pallas kernels: none -> 63.9 us  [per_device(): pl.pallas_call(functools.partial(kernel, blk_count, rep_count), out_shape...]
    dot_general x9 -> x0, matrix products: 49.6 us -> none  [the longest x3 18.2 us: tile_gradients(): lax.dot_general(misfit, pixel_rows, (((0,), (0,)), ((), ())), precision=l...]
    all_gather x3 -> x0, waiting for transfers between devices: 37.9 us -> none  [per_device(): scene_block = lax.all_gather(own_rows, 'rep', axis=0, tiled=True)]
    ppermute x3 -> x0, waiting for transfers between devices: 17.7 us -> none  [shifted(): return lax.ppermute(value, axis, pairs)]
    ppermute x3 -> x0, starting transfers between devices: 9.56 us -> none  [shifted(): return lax.ppermute(value, axis, pairs)]
    add x3 -> x0, other arithmetic: 3.19 us -> none  [per_device(): own_rows = own_rows + 8.0 / group_rows * grad_share]
    unnamed x13 -> x3, local copies, waits for them, and re-layouts: 4.38 us -> 5.64 us
  transfers between devices with their start and end apart: 9 -> 0, of which waited for: 9 -> 0; matrix products, arithmetic and copies ran while one was open for 7% -> 0% of each run, Pallas kernels for 0% -> 0%
where the time goes in v1:
time: 70.4 us; the launch traced here: 70.2 us
  Pallas kernels  63.9 us (91%)
  local copies, waits for them, and re-layouts  5.64 us (8%)
    pallas_call x1, Pallas kernels, per_device(): pl.pallas_call(functools.partial(kernel, blk_count, rep_count), out_shape...  63.9 us
    unnamed x3, local copies, waits for them, and re-layouts  5.64 us

profile of v1, /device:TPU:1, one launch (start us, length us, event | category | flops | bytes accessed | tf_op | source)
XLA Modules:
  0.0 70.2 jit_solution(13827630040958763871)
XLA Ops:
  0.6 1.3 %copy.7.occ_ref = s32[3,1]{1,0:T(4,128)} copy(s32[3,1]{0,1:T(1,128)} %param.9) | data formatting | bytes 24 | tf_op args[4]
  1.9 63.9 %shard_map.68 = (f32[768,256]{1,0:T(8,128)}, f32[1024,256]{1,0:T(8,128)}) custom-call(s32[3,1]{1,0:T(4,128)} %copy.7.occ_ref, f32[768,256]{1,0:T(8,128)} %pix_ref.1, f32[1024,256]{1,0:T(8,128)} %scene_ref.1, bf16[3,768,1024]{2,1,0:T(8,128)(2,1)} %elev_ref.1, bf16[3,768,1024]{2,1,0:T(8,128)(2,1)} %qual_ref.1), custom_call_target="tpu_custom_call" | custom-call | flops 10871635968 | bytes 12582912 | tf_op jit(solution)/shard_map/pallas_call | solution.py:266
  65.8 2.1 %copy.10 = f32[768,256]{1,0:T(8,128)} copy(f32[768,256]{1,0:T(8,128)} %get-tuple-element.4) | data formatting | bytes 1572864
  67.9 2.3 %copy.11 = f32[1024,256]{1,0:T(8,128)} copy(f32[1024,256]{1,0:T(8,128)} %get-tuple-element.5) | data formatting | bytes 2097152
